TPU v7x, 512 devices: a whole 4x8x8 slice. The times are simulated.
512 devices in a mesh: seq: 64 (over z, y), head: 8 (over x, core).
Axes of the slice: x: 4, y: 8, z: 8, core: 2. Of those that a mesh axis runs over, the one named last changes fastest.
Arguments:
- raw_keys: bfloat16 [2, 65536, 8, 128], P(None, 'seq', 'head'), may hold values from -6 to 6
- raw_values: bfloat16 [2, 65536, 8, 128], P(None, 'seq', 'head'), may hold values from -6 to 6
- phase: int32 [2], replicated, may hold values from 0 to 255, as said below
- ratio: int32 [2, 64], replicated, may hold values from 8 to 32, as said below
- resident_len: int32 [2, 64], replicated, may hold values from 1 to 256, as said below
- beacon_queries: bfloat16 [2, 8192, 8, 8, 128], P(None, 'seq', 'head'), may hold values from -150 to 150
- beacon_wk: bfloat16 [8192, 1024], P('seq', 'head'), may hold values from -0.125 to 0.125
- beacon_wv: bfloat16 [8192, 1024], P('seq', 'head'), may hold values from -0.125 to 0.125
- resident_keys: bfloat16 [2, 16384, 8, 128], P(None, 'seq', 'head'), may hold values from -6 to 6
- resident_values: bfloat16 [2, 16384, 8, 128], P(None, 'seq', 'head'), may hold values from -6 to 6
- decode_queries: bfloat16 [4, 2, 8, 8, 128], P(None, None, 'head'), may hold values from -150 to 150
- out_weight: bfloat16 [8192, 8192], P('head', 'seq'), may hold values from -0.0625 to 0.0625
Outputs:
- beacon_keys: bfloat16 [2, 8192, 8, 128], P(None, 'seq', 'head')
- beacon_values: bfloat16 [2, 8192, 8, 128], P(None, 'seq', 'head')
- projected: bfloat16 [4, 2, 8192], P(None, None, 'seq')
Inputs may be any that keep to these rules, and one draw needn't show every extreme that they name: `phase`: some request has 255. `ratio`: each value is 1024 // 128 times 1, 2 or 4; both ends occur. `resident_len`: some pair has 256.
All inputs are finite; a program needn't handle non-finite values.
Results may differ from a plain program's by a relative error of at most 0.025.
Values may be sent and summed in bfloat16 or wider, within the bound.
No kernel may reach another device: no remote copies, remote signals or barrier semaphores. Data moves between devices by JAX's collectives and lax.ppermute only.
A program may use at most 64 MiB of HBM per device.

v0:
```python
import math
import jax
import jax.numpy as jnp
from jax import lax
from jax.sharding import PartitionSpec as P

G = 8
INTERVAL = 1024
NB = 128
OFF = 256
STEPS = 4
masked_score = -1e30


def shifted(value, axis, steps):
    count = lax.axis_size(axis)
    first, last = (max(0, -steps), min(count, count - steps))
    return lax.ppermute(value, axis, [(source, source + steps) for source in range(first, last)])


def pool_part(queries, key_rows, value_rows, positions, present, reaches):
    inv_root = 1.0 / math.sqrt(queries.shape[-1])

    def per_request(members):
        query_block, key_block, value_block, position_row, present_row, reach_row = members
        scores = (
            jnp.einsum("jkgd,ikd->jkgi", query_block, key_block, preferred_element_type=jnp.float32)
            * inv_root
        )
        allowed = (
            present_row[None, :]
            & (position_row[None, :] >= 0)
            & (position_row[None, :] < INTERVAL)
            & (position_row[None, :] < reach_row[:, None])
        )
        cache_mask = allowed[:, None, None, :]
        row_peak = jnp.max(jnp.where(cache_mask, scores, masked_score), axis=-1)
        weights = jnp.where(cache_mask, jnp.exp(scores - row_peak[..., None]), 0.0)
        weight_sum = jnp.sum(weights, axis=-1)
        weighted = jnp.einsum(
            "jkgi,ikd->jkgd",
            weights.astype(jnp.bfloat16),
            value_block,
            preferred_element_type=jnp.float32,
        )
        return (row_peak, weight_sum, weighted)

    return lax.map(per_request, (queries, key_rows, value_rows, positions, present, reaches))


def body(
    raw_keys,
    raw_values,
    phase,
    ratio,
    resident_len,
    beacon_queries,
    beacon_wk,
    beacon_wv,
    resident_keys,
    resident_values,
    decode_queries,
    out_weight,
):
    requests = raw_keys.shape[0]
    kv_local = raw_keys.shape[2]
    head_dim = raw_keys.shape[3]
    shard_index = lax.axis_index("seq")
    shard_count = lax.axis_size("seq")
    is_first = shard_index == 0
    is_last = shard_index == shard_count - 1
    own_ratio = lax.dynamic_index_in_dim(ratio, shard_index, 1, keepdims=False)
    slot_ids = jnp.arange(NB, dtype=jnp.int32)
    lead_in = jnp.where(is_first, phase, 0)
    reaches = (slot_ids[None, :] + 1) * own_ratio[:, None] + lead_in[:, None]
    tail_keys = raw_keys[:, INTERVAL - OFF :]
    tail_values = raw_values[:, INTERVAL - OFF :]
    own_positions = jnp.arange(INTERVAL, dtype=jnp.int32)[None, :] + phase[:, None]
    rim_ids = jnp.arange(OFF, dtype=jnp.int32)
    rim_positions = rim_ids[None, :] - OFF + phase[:, None]
    near_keys, near_values = shifted((tail_keys, tail_values), "seq", 1)
    key_rows = jnp.concatenate([near_keys, raw_keys], axis=1)
    value_rows = jnp.concatenate([near_values, raw_values], axis=1)
    positions = jnp.concatenate([rim_positions, own_positions], axis=1)
    present = jnp.logical_not(is_first) | (positions >= phase[:, None])
    pooled_parts = pool_part(beacon_queries, key_rows, value_rows, positions, present, reaches)
    pooled = (pooled_parts[2] / pooled_parts[1][..., None]).astype(jnp.bfloat16)
    pooled_flat = pooled.reshape(requests * NB, kv_local * G * head_dim)
    pooled_whole = lax.all_gather(pooled_flat, "head", axis=1, tiled=True)
    key_sum = jnp.dot(
        pooled_whole,
        lax.all_gather(beacon_wk, "seq", axis=0, tiled=True),
        preferred_element_type=jnp.float32,
    )
    value_sum = jnp.dot(
        pooled_whole,
        lax.all_gather(beacon_wv, "seq", axis=0, tiled=True),
        preferred_element_type=jnp.float32,
    )
    made_keys = key_sum
    made_values = value_sum
    made_keys = made_keys.reshape(requests, NB, kv_local, head_dim)
    made_values = made_values.reshape(requests, NB, kv_local, head_dim)
    slot_live = slot_ids[None, :] < (INTERVAL // own_ratio)[:, None]
    beacon_keys = jnp.where(slot_live[:, :, None, None], made_keys, 0.0).astype(jnp.bfloat16)
    beacon_values = jnp.where(slot_live[:, :, None, None], made_values, 0.0).astype(jnp.bfloat16)
    cache_keys = jnp.concatenate([resident_keys, beacon_keys, tail_keys], axis=1)
    cache_values = jnp.concatenate([resident_values, beacon_values, tail_values], axis=1)
    own_len = lax.dynamic_index_in_dim(resident_len, shard_index, 1, keepdims=False)
    resident_ok = jnp.arange(resident_keys.shape[1], dtype=jnp.int32)[None, :] < own_len[:, None]
    leftover_ok = (rim_ids[None, :] >= OFF - phase[:, None]) & is_last
    usable = jnp.concatenate([resident_ok, slot_live, leftover_ok], axis=1)
    inv_root = 1.0 / math.sqrt(head_dim)
    scores = (
        jnp.einsum(
            "srkgd,rikd->rksgi", decode_queries, cache_keys, preferred_element_type=jnp.float32
        )
        * inv_root
    )
    cache_mask = usable[:, None, None, None, :]
    row_peak = jnp.max(jnp.where(cache_mask, scores, masked_score), axis=-1)
    weights = jnp.where(cache_mask, jnp.exp(scores - row_peak[..., None]), 0.0)
    weight_sum = jnp.sum(weights, axis=-1)
    weighted = jnp.einsum(
        "rksgi,rikd->rksgd",
        weights.astype(jnp.bfloat16),
        cache_values,
        preferred_element_type=jnp.float32,
    )
    global_peak = lax.pmax(row_peak, "seq")
    rescale = jnp.exp(row_peak - global_peak)
    total_sum, total_weighted = lax.psum(
        (weight_sum * rescale, weighted * rescale[..., None]), "seq"
    )
    attended = (total_weighted / total_sum[..., None]).astype(jnp.bfloat16)
    attended = jnp.transpose(attended, (2, 0, 1, 3, 4)).reshape(
        STEPS * requests, kv_local * G * head_dim
    )
    partial_value = jnp.dot(attended, out_weight, preferred_element_type=jnp.float32)
    summed = lax.psum(partial_value, "head")
    projected = summed.astype(jnp.bfloat16).reshape(STEPS, requests, out_weight.shape[1])
    return (beacon_keys, beacon_values, projected)


def solution(mesh):
    return jax.shard_map(
        body,
        mesh=mesh,
        in_specs=(
            P(None, "seq", "head", None),
            P(None, "seq", "head", None),
            P(),
            P(),
            P(),
            P(None, "seq", "head", None, None),
            P("seq", "head"),
            P("seq", "head"),
            P(None, "seq", "head", None),
            P(None, "seq", "head", None),
            P(None, None, "head", None, None),
            P("head", "seq"),
        ),
        out_specs=(
            P(None, "seq", "head", None),
            P(None, "seq", "head", None),
            P(None, None, "seq"),
        ),
        check_vma=False,
    )
```

profile of v0, /device:TPU:1, one launch (start us, length us, event | category | flops | bytes accessed | tf_op | source)
XLA Modules:
  0.0 666.6 jit_solution(5328392180371530264)
XLA Ops:
  7.2 1.0 slice.9
  8.2 4.7 collective-permute-start.1
  12.9 0.9 slice.8
  13.8 2.6 collective-permute-start
  17.9 1.2 copy.32
  20.6 1.0 fusion.44
  21.8 1.1 pad_maximum_fusion
  22.9 1.0 copy.31
  24.8 8.6 %while.12 = (s32[]{:T(128)}, f32[2,128,1,8]{1,3,2,0:T(8,128)S(1)}, f32[2,128,1,8,128]{1,4,3,2,0:T(8,128)S(1)}, pred[2,1280]{1,0:T(4,128)(4,1)S(1)}, s32[2,1280]{...) while((s32[]{:T(128)}, f32[2,128,1,8]{1,3,2,0:T(8,128)S(1)}, ...), condition=%wide.region_3.4_spmd, body=%wide.region_0.3_spmd.sunk | while | flops 685837312 | bytes 21023128 | solution.py:48
  24.9 0.9 compare_and_fusion.3
  26.8 1.2 fusion.67
  27.9 1.1 fusion.66
  29.2 0.9 compare_and_fusion.3
  31.1 1.2 fusion.67
  32.3 1.1 fusion.66
  33.8 0.9 copy.60
  35.8 64.2 %all-gather.6.cloned.1.call-done = bf16[8192,128]{1,0:T(8,128)(2,1)} async-done(((bf16[128,128]{1,0:T(8,128)(2,1)}), bf16[8192,128]{1,0:T(8,128)(2,1)}) %all-gather.6.cloned.1.call-update) | async-done | bytes 2097168 | tf_op jit(solution)/shard_map/all_gather | solution.py:92
  99.9 40.7 %all-gather.4.cloned.1.call-done = bf16[256,8192]{1,0:T(8,128)(2,1)} async-done(((bf16[256,1024]{1,0:T(8,128)(2,1)}), bf16[256,8192]{1,0:T(8,128)(2,1)}) %all-gather.4.cloned.1.call-update) | async-done | bytes 4194320 | tf_op jit(solution)/shard_map/all_gather | solution.py:89
  140.6 4.1 fusion.48
  144.8 78.4 %all-gather.8.cloned.1.call-done = bf16[8192,128]{1,0:T(8,128)(2,1)} async-done(((bf16[128,128]{1,0:T(8,128)(2,1)}), bf16[8192,128]{1,0:T(8,128)(2,1)}) %all-gather.8.cloned.1.call-update) | async-done | bytes 2097168 | tf_op jit(solution)/shard_map/all_gather | solution.py:97
  223.1 4.1 fusion.49
  227.9 113.3 %pmax.7 = f32[2,1,4,8]{3,2,0,1:T(4,128)S(1)} all-reduce(f32[2,1,4,8]{3,2,0,1:T(4,128)S(1)} %bitcast.153), channel_id=1, replica_groups=mesh['seq'=64,'head'=8] {'seq'}, use_global_device_ids=true, to_apply=%region_5.6 | all-reduce | flops 64 | bytes 512 | tf_op jit(solution)/shard_map/pmax | solution.py:130
  341.5 219.7 %all-reduce = (f32[2,1,4,8,128]{4,3,2,0,1:T(8,128)S(1)}, f32[2,4,8]{2,1,0:T(4,128)S(1)}) all-reduce(f32[2,1,4,8,128]{4,3,2,0,1:T(8,128)S(1)} %fusion.25, f32[2,4,8]{2,1,0:T(4,128)S(1)} %get-tuple-element.101), channel_id=1, replica_groups=mesh['seq'=64,'head'=8] {'seq'}, use_global_device_ids=true, to_apply=%region_6.7 | all-reduce | flops 8256 | bytes 66048 | tf_op jit(solution)/shard_map/psum | solution.py:132
  561.5 98.6 %psum.23 = bf16[8,128]{1,0:T(8,128)(2,1)} all-reduce(f32[8,128]{1,0:T(8,128)S(1)} %fusion.37), channel_id=1, replica_groups=mesh['seq'=64,'head'=8] {'head'}, use_global_device_ids=true, to_apply=%region_9.10 | all-reduce | flops 1024 | bytes 6144 | tf_op jit(solution)/shard_map/psum | solution.py:140
  (63 shorter events, 8.5 us)
Async XLA Ops:
  7.2 554.2 %copy-start = (bf16[1024,128]{1,0:T(8,128)(2,1)S(1)}, bf16[1024,128]{1,0:T(8,128)(2,1)}, u32[]{:S(2)}) copy-start(bf16[1024,128]{1,0:T(8,128)(2,1)} %param.25) | copy-start | bytes 786436
  7.2 17.6 %copy-start.1 = (bf16[2,128,1,8,128]{4,3,2,1,0:T(8,128)(2,1)S(1)}, bf16[2,128,1,8,128]{4,3,2,1,0:T(8,128)(2,1)}, u32[]{:S(2)}) copy-start(bf16[2,128,1,8,128]{4,3,2,1,0:T(8,128)(2,1)} %param.19) | copy-start | bytes 1572868
  7.2 92.7 %all-gather.6.cloned.1.call-start = ((), (), s32[]{:S(2)}) async-start(), calls=%async_computation.1 | async-start | bytes 2129920 | tf_op jit(solution)/shard_map/all_gather | solution.py:92
  8.2 14.6 %collective-permute-start.1 = (bf16[2,256,1,128]{3,1,0,2:T(8,128)(2,1)S(1)}, bf16[2,256,1,128]{3,1,0,2:T(8,128)(2,1)}, u32[]{:S(2)}, u32[]{:S(2)}) collective-permute-start(bf16[2,256,1,128]{3,1,0,2:T(8,128)(2,1)S(1)} %slice.9), channel_id=1, source_target_pairs={{0,8},{8,16},{16,24},{24,32},{32,40},{40,48},{48,56},{56,64},{64,7... | collective-permute-start | bytes 393224 | tf_op jit(solution)/shard_map/ppermute | solution.py:18
  13.8 7.9 %collective-permute-start = (bf16[2,256,1,128]{3,1,0,2:T(8,128)(2,1)S(1)}, bf16[2,256,1,128]{3,1,0,2:T(8,128)(2,1)S(1)}, u32[]{:S(2)}, u32[]{:S(2)}) collective-permute-start(bf16[2,256,1,128]{3,1,0,2:T(8,128)(2,1)S(1)} %slice.8), channel_id=1, source_target_pairs={{0,8},{8,16},{16,24},{24,32},{32,40},{40,48},{48,56},{56,64},{64,7... | collective-permute-start | bytes 393224 | tf_op jit(solution)/shard_map/ppermute | solution.py:18
  16.4 124.2 %all-gather.4.cloned.1.call-start = ((), (), s32[]{:S(2)}) async-start(), calls=%async_computation | async-start | bytes 4718592 | tf_op jit(solution)/shard_map/all_gather | solution.py:89
  24.8 2.0 copy-start.2
  29.1 2.0 copy-start.2
  34.8 188.4 %all-gather.8.cloned.1.call-start = ((), (), s32[]{:S(2)}) async-start(), calls=%async_computation.2 | async-start | bytes 2129920 | tf_op jit(solution)/shard_map/all_gather | solution.py:97
  144.7 82.6 %copy-start.5 = (bf16[2,256,1,128]{3,1,2,0:T(8,128)(2,1)S(1)}, bf16[2,256,1,128]{3,1,2,0:T(8,128)(2,1)}, u32[]{:S(2)}) copy-start(bf16[2,256,1,128]{3,1,2,0:T(8,128)(2,1)} %param.22) | copy-start | bytes 393220
  144.8 82.6 %copy-start.7 = (bf16[4,2,1,8,128]{4,3,2,1,0:T(8,128)(2,1)S(1)}, bf16[4,2,1,8,128]{4,3,2,1,0:T(8,128)(2,1)}, u32[]{:S(2)}) copy-start(bf16[4,2,1,8,128]{4,3,2,1,0:T(8,128)(2,1)} %param.24) | copy-start | bytes 49156
  144.8 196.5 %copy-start.6 = (bf16[2,256,1,128]{3,1,2,0:T(8,128)(2,1)S(1)}, bf16[2,256,1,128]{3,1,2,0:T(8,128)(2,1)}, u32[]{:S(2)}) copy-start(bf16[2,256,1,128]{3,1,2,0:T(8,128)(2,1)} %param.23) | copy-start | bytes 393220
  227.4 432.7 %copy-start.3 = (bf16[2,128,1,128]{3,1,0,2:T(8,128)(2,1)}, bf16[2,128,1,128]{3,1,0,2:T(8,128)(2,1)S(1)}, u32[]{:S(2)}) copy-start(bf16[2,128,1,128]{3,1,0,2:T(8,128)(2,1)S(1)} %get-tuple-element.105) | copy-start | bytes 196612
  227.4 432.7 %copy-start.4 = (bf16[2,128,1,128]{3,1,0,2:T(8,128)(2,1)}, bf16[2,128,1,128]{3,1,0,2:T(8,128)(2,1)S(1)}, u32[]{:S(2)}) copy-start(bf16[2,128,1,128]{3,1,0,2:T(8,128)(2,1)S(1)} %get-tuple-element.106) | copy-start | bytes 196612
Sparse Core Ops, SparseCore 0:
  16.6 83.3 all-gather.5
  102.0 38.5 all-gather.3
  143.7 79.3 all-gather.7
where the time goes:
time: 667 us
  blocking collectives  432 us (65%)
  waiting for transfers between devices  184 us (28%)
  between operations  14 us (2%)
  matrix products  13.1 us (2%)
  other arithmetic  10.8 us (2%)
  starting transfers between devices  7.38 us (1%)
    psum x1, blocking collectives, body(): lax.psum((weight_sum * rescale, weighted * rescale[..., None]), 'seq')  220 us
    pmax x1, blocking collectives, body(): global_peak = lax.pmax(row_peak, 'seq')  113 us
    psum x1, blocking collectives, body(): summed = lax.psum(partial_value, 'head')  98.6 us
    all_gather x1, waiting for transfers between devices, body(): lax.all_gather(beacon_wv, 'seq', axis=0, tiled=True)  78.4 us
    all_gather x1, waiting for transfers between devices, body(): lax.all_gather(beacon_wk, 'seq', axis=0, tiled=True)  64.2 us
    all_gather x1, waiting for transfers between devices, body(): pooled_whole = lax.all_gather(pooled_flat, 'head', axis=1, tiled=True)  40.7 us
  transfers between devices with their start and end apart: 5, of which 3 were waited for; matrix products, arithmetic and copies ran while one was open for 3% of the time, Pallas kernels for 0%

commit v1 on v0

--- a/solution.py
+++ b/solution.py
@@ -94,7 +94,9 @@
     )
     value_sum = jnp.dot(
         pooled_whole,
-        lax.all_gather(beacon_wv, "seq", axis=0, tiled=True),
+        jnp.concatenate(
+            lax.all_to_all(jnp.stack([beacon_wv] * lax.axis_size("seq")), "seq", 0, 0), axis=0
+        ),
         preferred_element_type=jnp.float32,
     )
     made_keys = key_sum

time: 667 us -> 629 us (0.943)
  waiting for transfers between devices: 184 us -> 130 us
  starting transfers between devices: 7.38 us -> 21.8 us
    all_gather x1 -> x0, waiting for transfers between devices: 78.4 us -> none  [body(): lax.all_gather(beacon_wv, 'seq', axis=0, tiled=True)]
    all_gather x1, waiting for transfers between devices: 64.2 us -> 89.5 us  [body(): lax.all_gather(beacon_wk, 'seq', axis=0, tiled=True)]
    all_to_all x0 -> x1, starting transfers between devices: none -> 14.5 us  [body(): lax.all_to_all(jnp.stack([beacon_wv] * lax.axis_size('seq')), 'seq', 0, 0)]
  transfers between devices with their start and end apart: 5 -> 5, of which waited for: 3 -> 2; matrix products, arithmetic and copies ran while one was open for 3% -> 4% of each run, Pallas kernels for 0% -> 0%
where the time goes in v1:
time: 629 us
  blocking collectives  431 us (69%)
  waiting for transfers between devices  130 us (21%)
  starting transfers between devices  21.8 us (3%)
  between operations  14.3 us (2%)
  matrix products  12.4 us (2%)
  other arithmetic  11.6 us (2%)
  local copies, waits for them, and re-layouts  7.48 us (1%)
    psum x1, blocking collectives, body(): lax.psum((weight_sum * rescale, weighted * rescale[..., None]), 'seq')  220 us
    pmax x1, blocking collectives, body(): global_peak = lax.pmax(row_peak, 'seq')  117 us
    psum x1, blocking collectives, body(): summed = lax.psum(partial_value, 'head')  94.2 us
    all_gather x1, waiting for transfers between devices, body(): lax.all_gather(beacon_wk, 'seq', axis=0, tiled=True)  89.5 us
    all_gather x1, waiting for transfers between devices, body(): pooled_whole = lax.all_gather(pooled_flat, 'head', axis=1, tiled=True)  40.7 us
    all_to_all x1, starting transfers between devices, body(): lax.all_to_all(jnp.stack([beacon_wv] * lax.axis_size('seq')), 'seq', 0, 0)  14.5 us
  transfers between devices with their start and end apart: 5, of which 2 were waited for; matrix products, arithmetic and copies ran while one was open for 4% of the time, Pallas kernels for 0%

profile of v1, /device:TPU:1, one launch (start us, length us, event | category | flops | bytes accessed | tf_op | source)
XLA Modules:
  0.0 628.6 jit_solution(13770961011729380721)
XLA Ops:
  7.2 1.0 slice.9
  8.2 4.7 collective-permute-start.1
  13.8 2.6 collective-permute-start
  17.9 1.2 copy.32
  20.6 1.0 fusion.45
  21.8 1.1 pad_maximum_fusion
  22.9 1.0 copy.31
  24.8 8.6 %while.12 = (s32[]{:T(128)}, f32[2,128,1,8]{1,3,2,0:T(8,128)S(1)}, f32[2,128,1,8,128]{1,4,3,2,0:T(8,128)S(1)}, pred[2,1280]{1,0:T(4,128)(4,1)S(1)}, s32[2,1280]{...) while((s32[]{:T(128)}, f32[2,128,1,8]{1,3,2,0:T(8,128)S(1)}, ...), condition=%wide.region_3.4_spmd, body=%wide.region_0.3_spmd.sunk | while | flops 685837312 | bytes 21023128 | solution.py:48
  24.9 0.9 compare_and_fusion.3
  26.8 1.2 fusion.68
  27.9 1.1 fusion.67
  29.2 0.9 compare_and_fusion.3
  31.1 1.2 fusion.68
  32.3 1.1 fusion.67
  33.8 0.9 copy.60
  34.8 1.9 stack.2
  36.7 14.5 %all-to-all-start = ((bf16[64,128,128]{2,1,0:T(8,128)(2,1)}), bf16[64,128,128]{2,1,0:T(8,128)(2,1)S(1)}, u32[]{:S(2)}, u32[]{:S(2)}) async-start(bf16[64,128,128]{2,1,0:T(8,128)(2,1)} %stack.2), calls=%async_computation | async-start | bytes 4194304 | tf_op jit(solution)/shard_map/all_to_all | solution.py:98
  51.4 89.5 %all-gather.5.cloned.1.call-done = bf16[8192,128]{1,0:T(8,128)(2,1)} async-done(((bf16[128,128]{1,0:T(8,128)(2,1)}), bf16[8192,128]{1,0:T(8,128)(2,1)}) %all-gather.5.cloned.1.call-update) | async-done | bytes 2097168 | tf_op jit(solution)/shard_map/all_gather | solution.py:92
  140.9 40.7 %all-gather.3.cloned.1.call-done = bf16[256,8192]{1,0:T(8,128)(2,1)} async-done(((bf16[256,1024]{1,0:T(8,128)(2,1)}), bf16[256,8192]{1,0:T(8,128)(2,1)}) %all-gather.3.cloned.1.call-update) | async-done | bytes 4194320 | tf_op jit(solution)/shard_map/all_gather | solution.py:89
  181.6 4.1 fusion.49
  186.2 116.8 %pmax.7 = f32[2,1,4,8]{3,2,0,1:T(4,128)S(1)} all-reduce(f32[2,1,4,8]{3,2,0,1:T(4,128)S(1)} %bitcast.161), channel_id=1, replica_groups=mesh['seq'=64,'head'=8] {'seq'}, use_global_device_ids=true, to_apply=%region_5.6 | all-reduce | flops 64 | bytes 512 | tf_op jit(solution)/shard_map/pmax | solution.py:132
  303.9 3.4 fusion.25
  307.6 219.7 %all-reduce = (f32[2,1,4,8,128]{4,3,2,0,1:T(8,128)S(1)}, f32[2,4,8]{2,1,0:T(4,128)S(1)}) all-reduce(f32[2,1,4,8,128]{4,3,2,0,1:T(8,128)S(1)} %fusion.26, f32[2,4,8]{2,1,0:T(4,128)S(1)} %get-tuple-element.101), channel_id=1, replica_groups=mesh['seq'=64,'head'=8] {'seq'}, use_global_device_ids=true, to_apply=%region_6.7 | all-reduce | flops 8256 | bytes 66048 | tf_op jit(solution)/shard_map/psum | solution.py:134
  527.6 94.2 %psum.23 = bf16[8,128]{1,0:T(8,128)(2,1)} all-reduce(f32[8,128]{1,0:T(8,128)S(1)} %fusion.38), channel_id=1, replica_groups=mesh['seq'=64,'head'=8] {'head'}, use_global_device_ids=true, to_apply=%region_9.10 | all-reduce | flops 1024 | bytes 6144 | tf_op jit(solution)/shard_map/psum | solution.py:142
  (64 shorter events, 9.4 us)
Async XLA Ops:
  7.2 520.3 %copy-start = (bf16[1024,128]{1,0:T(8,128)(2,1)S(1)}, bf16[1024,128]{1,0:T(8,128)(2,1)}, u32[]{:S(2)}) copy-start(bf16[1024,128]{1,0:T(8,128)(2,1)} %param.25) | copy-start | bytes 786436
  7.2 17.6 %copy-start.1 = (bf16[2,128,1,8,128]{4,3,2,1,0:T(8,128)(2,1)S(1)}, bf16[2,128,1,8,128]{4,3,2,1,0:T(8,128)(2,1)}, u32[]{:S(2)}) copy-start(bf16[2,128,1,8,128]{4,3,2,1,0:T(8,128)(2,1)} %param.19) | copy-start | bytes 1572868
  7.2 133.7 %all-gather.5.cloned.1.call-start = ((), (), s32[]{:S(2)}) async-start(), calls=%async_computation.2 | async-start | bytes 2129920 | tf_op jit(solution)/shard_map/all_gather | solution.py:92
  8.2 14.6 %collective-permute-start.1 = (bf16[2,256,1,128]{3,1,0,2:T(8,128)(2,1)S(1)}, bf16[2,256,1,128]{3,1,0,2:T(8,128)(2,1)}, u32[]{:S(2)}, u32[]{:S(2)}) collective-permute-start(bf16[2,256,1,128]{3,1,0,2:T(8,128)(2,1)S(1)} %slice.9), channel_id=1, source_target_pairs={{0,8},{8,16},{16,24},{24,32},{32,40},{40,48},{48,56},{56,64},{64,7... | collective-permute-start | bytes 393224 | tf_op jit(solution)/shard_map/ppermute | solution.py:18
  13.8 7.9 %collective-permute-start = (bf16[2,256,1,128]{3,1,0,2:T(8,128)(2,1)S(1)}, bf16[2,256,1,128]{3,1,0,2:T(8,128)(2,1)S(1)}, u32[]{:S(2)}, u32[]{:S(2)}) collective-permute-start(bf16[2,256,1,128]{3,1,0,2:T(8,128)(2,1)S(1)} %slice.8), channel_id=1, source_target_pairs={{0,8},{8,16},{16,24},{24,32},{32,40},{40,48},{48,56},{56,64},{64,7... | collective-permute-start | bytes 393224 | tf_op jit(solution)/shard_map/ppermute | solution.py:18
  16.4 165.2 %all-gather.3.cloned.1.call-start = ((), (), s32[]{:S(2)}) async-start(), calls=%async_computation.1 | async-start | bytes 4718592 | tf_op jit(solution)/shard_map/all_gather | solution.py:89
  24.8 2.0 copy-start.2
  29.1 2.0 copy-start.2
  33.4 1.4 copy-start.4
  36.7 267.2 %all-to-all-start = ((bf16[64,128,128]{2,1,0:T(8,128)(2,1)}), bf16[64,128,128]{2,1,0:T(8,128)(2,1)S(1)}, u32[]{:S(2)}, u32[]{:S(2)}) async-start(bf16[64,128,128]{2,1,0:T(8,128)(2,1)} %stack.2), calls=%async_computation | async-start | bytes 4194304 | tf_op jit(solution)/shard_map/all_to_all | solution.py:98
  51.2 134.7 %copy-start.5 = (bf16[2,256,1,128]{3,1,2,0:T(8,128)(2,1)S(1)}, bf16[2,256,1,128]{3,1,2,0:T(8,128)(2,1)}, u32[]{:S(2)}) copy-start(bf16[2,256,1,128]{3,1,2,0:T(8,128)(2,1)} %param.22) | copy-start | bytes 393220
  51.2 134.7 %copy-start.7 = (bf16[4,2,1,8,128]{4,3,2,1,0:T(8,128)(2,1)S(1)}, bf16[4,2,1,8,128]{4,3,2,1,0:T(8,128)(2,1)}, u32[]{:S(2)}) copy-start(bf16[4,2,1,8,128]{4,3,2,1,0:T(8,128)(2,1)} %param.24) | copy-start | bytes 49156
  185.7 121.6 %copy-start.6 = (bf16[2,256,1,128]{3,1,2,0:T(8,128)(2,1)S(1)}, bf16[2,256,1,128]{3,1,2,0:T(8,128)(2,1)}, u32[]{:S(2)}) copy-start(bf16[2,256,1,128]{3,1,2,0:T(8,128)(2,1)} %param.23) | copy-start | bytes 393220
  307.3 314.5 %copy-start.3 = (bf16[2,128,128]{2,1,0:T(8,128)(2,1)}, bf16[2,128,128]{2,1,0:T(8,128)(2,1)S(1)}, u32[]{:S(2)}) copy-start(bf16[2,128,128]{2,1,0:T(8,128)(2,1)S(1)} %fusion.25) | copy-start | bytes 196612
Sparse Core Ops, SparseCore 0:
  16.6 124.2 all-gather.4
  143.0 38.5 all-gather.2
